TPU v7x, 128 devices: a whole 4x4x4 slice. The times are simulated.
128 devices in a mesh: row: 16 (over z_lo, x, core), col: 8 (over y, z_hi).
Axes of the slice: x: 4, y: 4, z: 4 (z_hi: 2, z_lo: 2; z = z_hi * 2 + z_lo), core: 2. Of those that a mesh axis runs over, the one named last changes fastest.
Arguments:
- crossings: bfloat16 [6144, 2, 128, 128], P(('row', 'col')), may hold values from -50 to 50
- counts: int32 [8, 16], P('col', 'row'), may hold values from 1 to 48, 192 in all within a row
- dest: int32 [128, 48], P(('row', 'col')), may hold values from 0 to 47, each once within a row
Outputs:
- scores: float32 [1536, 1536], P('row', 'col')
Inputs may be any that keep to these rules, and one draw needn't show every extreme that they name: In every column c the counts add up to 192, and one shard of every column holds exactly 48. `dest`: each shard's row is a permutation.
All inputs are finite; a program needn't handle non-finite values.
Results may differ from a plain program's by a relative error of at most 0.00075.
Values may be sent and summed in bfloat16 or wider, within the bound.
A program may use at most 192 MiB of HBM per device.

v0:
```python
import math

import jax
import jax.numpy as jnp
import ml_dtypes
import numpy as np
from jax import lax
from jax.experimental import pallas as pl
from jax.experimental.pallas import tpu as pltpu
from jax.sharding import PartitionSpec as P

M = 12
NX = 128
ENTRIES = 256
ROWS = 16
COLS = 8
BUCKETS = 3
PARTS = 8
PITCH = 200

epsilon = 1e-06

MESH = pl.DeviceIdType.MESH
NT = (((1,), (1,)), ((), ()))
f32 = jnp.float32
bf16 = jnp.bfloat16


def split3(table):
    high = table.astype(ml_dtypes.bfloat16)
    rest = table - high.astype(np.float64)
    mid = rest.astype(ml_dtypes.bfloat16)
    low = (rest - mid.astype(np.float64)).astype(ml_dtypes.bfloat16)
    return high, mid, low


def tables():
    rows = np.arange(NX)
    part, inner = rows // 16, rows % 16
    wave = part * 8 + inner % 8
    imaginary = (inner >= 8) & (wave > 0)
    wave = np.where((inner >= 8) & (wave == 0), NX // 2, wave)
    points = np.arange(NX)
    angles = 2.0 * math.pi * ((wave[:, None] * points[None, :]) % NX) / NX
    forward = np.where(imaginary[:, None], -np.sin(angles), np.cos(angles))
    weight = np.where((wave == 0) | (wave == NX // 2), 1.0, 2.0)[:, None]
    inverse = weight * np.where(imaginary[:, None], -np.sin(angles), np.cos(angles)) / NX
    inverse = inverse - inverse.mean(1, keepdims=True)
    f_high, f_mid, f_low = split3(forward)
    forward_stack = np.concatenate([f_high, f_mid, f_low], 0)
    i_high, i_mid, _ = split3(inverse.T)
    shift = np.block([[i_high, i_high], [i_mid, np.zeros_like(i_mid)]])
    swap = np.zeros((256, 256))
    for first in range(16):
        for second in range(16):
            swap[first * 16 + second, second * 16 + first] = 1.0
    mirror = np.zeros((ENTRIES, ENTRIES))
    for point in range(128):
        mirror[(-point) % 128, point] = 1.0
        mirror[128 + (-point) % 128, 128 + point] = -1.0
    return (
        forward_stack.astype(ml_dtypes.bfloat16),
        swap.astype(ml_dtypes.bfloat16),
        mirror.astype(ml_dtypes.bfloat16),
        shift.astype(ml_dtypes.bfloat16),
    )


def dot_nt(a, b):
    return lax.dot_general(a, b, NT, preferred_element_type=f32)


def place():
    r = lax.axis_index("row")
    c = lax.axis_index("col")
    return r // 8, (r // 2) % 4, r % 2, c // 2, c % 2


def score_kernel(
    picks, planes, forward, swap, mirror, shift, out,
    cols, leads, y_lead, y_col, gram_a, gram_b, e_lead, e_col, send, recv,
):
    z, x, k, y, h = place()
    my_row = z * 8 + x * 2 + k
    my_col = y * 2 + h

    def row_at(dz, dx, dk=0):
        return ((z + dz) % 2) * 8 + ((x + dx) % 4) * 2 + (k + dk) % 2

    def col_at(dh, dy):
        return ((y + dy) % 4) * 2 + (h + dh) % 2

    sib, zl = (row_at(0, 0, 1), my_col), (row_at(1, 0), my_col)
    xp, xm = (row_at(0, 1), my_col), (row_at(0, 3), my_col)
    zh, yp, ym = (my_row, col_at(1, 0)), (my_row, col_at(0, 1)), (my_row, col_at(0, 3))

    barrier = pltpu.get_barrier_semaphore()
    for device in (sib, zl, xp, xm, zh, yp, ym):
        pl.semaphore_signal(barrier, inc=1, device_id=device, device_id_type=MESH)
    pl.semaphore_wait(barrier, 7)

    def transform(p, _):
        parts = dot_nt(forward[...], planes[picks[p]])
        value = (parts[:NX] + (parts[NX : 2 * NX] + parts[2 * NX :])).astype(bf16)
        cols[my_row, p] = value
        leads[my_col, p] = value
        return 0

    lax.fori_loop(0, M, transform, 0)

    def piece(ref, slot, t):
        return ref.at[slot, :, pl.ds(pl.multiple_of(t * 16, 16), 16), :]

    def copy(flow, ref, slot, t, device):
        block = piece(ref, slot, t)
        return pltpu.make_async_remote_copy(
            src_ref=block,
            dst_ref=block,
            send_sem=send.at[flow, t],
            recv_sem=recv.at[flow, t],
            device_id=device,
            device_id_type=MESH,
        )

    own_c, own_l = row_at(0, 0), col_at(0, 0)
    sends = {
        0: (cols, own_c, zl), 1: (cols, own_c, xp), 3: (cols, own_c, xm), 7: (cols, own_c, sib),
        2: (cols, row_at(1, 0), xp), 4: (cols, row_at(1, 0), xm), 8: (cols, row_at(1, 0), sib),
        5: (cols, row_at(0, 3), xp), 9: (cols, row_at(0, 3), sib), 10: (cols, row_at(1, 3), sib),
        11: (cols, row_at(0, 1), sib), 6: (cols, row_at(1, 1), xm), 12: (cols, row_at(1, 1), sib),
        13: (cols, row_at(0, 2), sib), 14: (cols, row_at(1, 2), sib),
        15: (leads, own_l, zh), 16: (leads, own_l, yp), 18: (leads, own_l, ym),
        17: (leads, col_at(1, 0), yp), 19: (leads, col_at(1, 0), ym),
        20: (leads, col_at(0, 3), yp), 21: (leads, col_at(1, 1), ym),
    }
    arrives = {
        0: row_at(1, 0), 1: row_at(0, 3), 2: row_at(1, 3), 3: row_at(0, 1), 4: row_at(1, 1),
        5: row_at(0, 2), 6: row_at(1, 2),
        7: row_at(0, 0, 1), 8: row_at(1, 0, 1), 9: row_at(0, 3, 1), 10: row_at(1, 3, 1),
        11: row_at(0, 1, 1), 12: row_at(1, 1, 1), 13: row_at(0, 2, 1), 14: row_at(1, 2, 1),
        15: col_at(1, 0), 16: col_at(0, 3), 17: col_at(1, 3), 18: col_at(0, 1), 19: col_at(1, 1),
        20: col_at(0, 2), 21: col_at(1, 2),
    }

    def start(flows, t):
        for flow in flows:
            ref, slot, device = sends[flow]
            copy(flow, ref, slot, t, device).start()

    def wait_in(flows, t):
        for flow in flows:
            ref, _, device = sends[flow]
            copy(flow, ref, arrives[flow], t, device).wait_recv()

    e_lead[...] = jnp.zeros_like(e_lead)
    e_col[...] = jnp.zeros_like(e_col)

    def score_part(t):
        r0 = pl.ds(pl.multiple_of(t * 16, 16), 16)
        order = swap[...]

        def relay(ref, groups, dst):
            flat = ref.reshape(groups * 16, NX, ENTRIES)
            for g in range(groups):
                block = flat[g * 16 : (g + 1) * 16, r0, :].reshape(256, ENTRIES)
                turned = jnp.dot(order, block, preferred_element_type=f32).astype(bf16)
                dst[:, g * 16 : (g + 1) * 16, :] = turned.reshape(16, 16, ENTRIES)

        relay(leads, 6, y_lead)
        relay(cols, 12, y_col)
        first = jnp.where(t == 0, 1.0, 0.0).astype(f32)
        for dst, source, count in ((e_lead, y_lead, 96), (e_col, y_col, 192)):
            total = dst[...]
            for j in range(16):
                value = source[j, :count, :].astype(f32)
                square = value * value
                square = square[:, :128] + square[:, 128:]
                weight = (2.0 - first) if j % 8 == 0 else 2.0
                total = total + weight * square
            dst[...] = total
        turn = mirror[...]
        for j in range(16):
            y_lead[j, 96:, :] = jnp.dot(y_lead[j, :96, :], turn, preferred_element_type=f32).astype(bf16)
        for i in range(8):
            lr, li, tr, ti = y_lead[i], y_lead[8 + i], y_col[i], y_col[8 + i]
            rr, ii, ri, ir = dot_nt(lr, tr), dot_nt(li, ti), dot_nt(lr, ti), dot_nt(li, tr)
            if i == 0:
                real = rr + (1.0 - first) * ii
                imag = first * ii + (1.0 - first) * (ri - ir)
            else:
                real, imag = rr + ii, ri - ir
            for value, j in ((real, i), (imag, 8 + i)):
                base = pl.ds(pl.multiple_of((t * 16 + j) * PITCH, 8), 192)
                gram_a[base, :] = value[:, :128]
                gram_b[base, :64] = value[:, 128:]

    def step(s, _):
        @pl.when(s < PARTS)
        def _():
            start((0, 1, 3, 15, 16, 18, 7), s)

        @pl.when((s >= 1) & (s < PARTS + 1))
        def _():
            wait_in((0, 15), s - 1)
            start((2, 4, 17, 19, 8), s - 1)

        @pl.when((s >= 2) & (s < PARTS + 2))
        def _():
            wait_in((1, 4, 16, 19), s - 2)
            start((5, 6, 20, 21, 9, 12), s - 2)
            wait_in((2, 3), s - 2)
            start((10, 11), s - 2)

        @pl.when((s >= 3) & (s < PARTS + 3))
        def _():
            wait_in((5, 6), s - 3)
            start((13, 14), s - 3)

        @pl.when(s >= 4)
        def _():
            wait_in((17, 18, 20, 21, 7, 8, 9, 10, 11, 12, 13, 14), s - 4)
            score_part(s - 4)

        return 0

    lax.fori_loop(0, PARTS + 4, step, 0)

    scale_lead = jnp.sqrt(jnp.sum(e_lead[...], -1, keepdims=True) / (NX * NX * ENTRIES) + epsilon)
    ones = jnp.ones((8, 128), f32)
    across = lax.dot_general(ones, e_col[...], NT, precision=lax.Precision.HIGHEST, preferred_element_type=f32)
    scale_col = jnp.sqrt(across[:1] / (NX * NX * ENTRIES) + epsilon)
    e_lead[...] = jnp.broadcast_to(scale_lead, (96, 128))
    to_shift = shift[...]

    def best(b, _):
        found = []
        for u in range(8):
            a = b * 8 + u
            values = []
            for start_row in (a, a + 96):
                values.append(gram_a[pl.ds(start_row, NX, stride=PITCH), :])
                values.append(gram_b[pl.ds(start_row, NX, stride=PITCH), :][:, :64])
            value = jnp.concatenate(values, 1)
            high = value.astype(bf16)
            low = (value - high.astype(f32)).astype(bf16)
            moved = jnp.dot(to_shift, jnp.concatenate([high, low], 0), preferred_element_type=f32)
            top = jnp.max(moved[:NX] + moved[NX:], axis=0, keepdims=True)
            found.append(jnp.maximum(top[:, :192], top[:, 192:]))
        rows = pl.ds(pl.multiple_of(b * 8, 8), 8)
        scale = e_lead[rows, :]
        scale = jnp.concatenate([scale, scale[:, :64]], 1)
        out[rows, :] = jnp.concatenate(found, 0) / (math.sqrt(NX * ENTRIES) * scale * scale_col)
        return 0

    lax.fori_loop(0, 96 // 8, best, 0)

    def finish(t, _):
        for flow, (ref, slot, device) in sends.items():
            copy(flow, ref, slot, t, device).wait_send()
        return 0

    lax.fori_loop(0, PARTS, finish, 0)


def scores_of(picks, planes):
    vmem = pl.BlockSpec(memory_space=pltpu.VMEM)
    return pl.pallas_call(
        score_kernel,
        out_shape=jax.ShapeDtypeStruct((COLS * M, ROWS * M), f32),
        in_specs=[pl.BlockSpec(memory_space=pltpu.SMEM)] + [vmem] * 5,
        out_specs=vmem,
        scratch_shapes=[
            pltpu.VMEM((ROWS, M, NX, ENTRIES), bf16),
            pltpu.VMEM((COLS, M, NX, ENTRIES), bf16),
            pltpu.VMEM((16, 192, ENTRIES), bf16),
            pltpu.VMEM((16, 192, ENTRIES), bf16),
            pltpu.VMEM((NX * PITCH, 128), f32),
            pltpu.VMEM((NX * PITCH, 128), f32),
            pltpu.VMEM((96, 128), f32),
            pltpu.VMEM((192, 128), f32),
            pltpu.SemaphoreType.DMA((22, PARTS)),
            pltpu.SemaphoreType.DMA((22, PARTS)),
        ],
        compiler_params=pltpu.CompilerParams(
            collective_id=1, has_side_effects=True, vmem_limit_bytes=60 * 2**20
        ),
        name="scores",
    )(picks, planes, *[jnp.asarray(table) for table in tables()])


def body(crossings, counts, dest):
    my_row = lax.axis_index("row")
    slot_total = crossings.shape[0]
    shard_counts = lax.all_gather(counts, "row", axis=1, tiled=True).reshape(ROWS)
    source_ids = jnp.arange(ROWS, dtype=jnp.int32)
    offsets = jnp.sum(jnp.where(source_ids[None, :] < source_ids[:, None], shard_counts[None, :], 0), 1)
    my_offset = jnp.sum(jnp.where(source_ids < my_row, shard_counts, 0))
    slot_ids = jnp.arange(slot_total, dtype=jnp.int32)
    buckets = jnp.arange(BUCKETS, dtype=jnp.int32)[None, :]
    outgoing = (buckets * ROWS + (source_ids[:, None] - my_offset) % ROWS).reshape(-1)
    chosen = jnp.sum(jnp.where(dest.reshape(1, -1) == outgoing[:, None], slot_ids[None, :], 0), 1)
    payload = crossings.reshape(slot_total, -1)[chosen].reshape(ROWS, BUCKETS, ENTRIES, NX)
    received = lax.all_to_all(payload, "row", split_axis=0, concat_axis=0, tiled=True)
    wanted = jnp.arange(M, dtype=jnp.int32)[:, None] * ROWS + my_row
    within = wanted - offsets[None, :]
    hit = (within >= 0) & (within < shard_counts[None, :])
    picks = jnp.sum(jnp.where(hit, source_ids[None, :] * BUCKETS + within // ROWS, 0), 1)
    return scores_of(picks, received.reshape(slot_total, ENTRIES, NX))


def solution(mesh):
    return jax.shard_map(
        body,
        mesh=mesh,
        in_specs=(P(("row", "col"), None, None, None), P("col", "row"), P(("row", "col"), None)),
        out_specs=P("row", "col"),
        check_vma=False,
    )
```

profile of v0, /device:TPU:1, one launch (start us, length us, event | category | flops | bytes accessed | tf_op | source)
XLA Modules:
  0.0 166.8 jit_solution(6421155713368742583)
XLA Ops:
  0.7 1.2 dynamic-slice
  1.9 0.7 bitcast_dynamic-update-slice_fusion
  2.6 11.2 %all-reduce = s32[16]{0:T(128)S(1)} all-reduce(s32[16]{0:T(128)S(1)} %bitcast_dynamic-update-slice_fusion), channel_id=1, replica_groups=mesh['row'=16,'col'=8] {'row'}, use_global_device_ids=true, to_apply=%add | all-reduce | flops 16 | bytes 128 | tf_op jit(solution)/shard_map/jit(_where)/broadcast_in_dim | solution.py:296
  13.8 0.6 fusion.9
  14.4 0.7 and_select_fusion
  15.0 0.1 broadcast_add_fusion
  15.1 0.1 add.72
  15.2 0.8 select_reduce_fusion
  16.1 3.9 %copy.11 = bf16[6,8,256,128]{3,1,2,0:T(8,128)(2,1)S(1)} copy(bf16[6,8,256,128]{3,2,1,0:T(8,128)(2,1)} %bitcast.21) | data formatting | bytes 6291456
  20.0 4.3 %gather_fusion = bf16[48,32768]{1,0:T(8,128)(2,1)} fusion(bf16[48,32768]{1,0:T(8,128)(2,1)S(1)} %bitcast.17, s32[1024]{0:T(1024)S(1)} %pad_clamp_fusion), kind=kCustom, calls=%fused_computation | custom fusion | bytes 6291648 | tf_op jit(solution)/shard_map/gather | solution.py:302
  24.3 4.4 %copy.9 = bf16[6,8,256,128]{3,2,1,0:T(8,128)(2,1)} copy(bf16[6,8,256,128]{3,1,2,0:T(8,128)(2,1)} %bitcast.20) | data formatting | bytes 6291456
  28.7 6.6 %all-to-all-start = ((bf16[16,3,256,128]{3,2,1,0:T(8,128)(2,1)}), bf16[16,3,256,128]{3,2,1,0:T(8,128)(2,1)S(1)}, u32[]{:S(2)}, u32[]{:S(2)}) async-start(bf16[16,3,256,128]{3,2,1,0:T(8,128)(2,1)} %bitcast.19), calls=%async_computation | async-start | bytes 6291456 | tf_op jit(solution)/shard_map/all_to_all | solution.py:303
  35.3 0.1 select_reduce_fusion.1
  35.4 0.7 fusion.3.picks
  36.1 41.0 %all-to-all-done = bf16[16,3,256,128]{3,2,1,0:T(8,128)(2,1)S(1)} async-done(((bf16[16,3,256,128]{3,2,1,0:T(8,128)(2,1)}), bf16[16,3,256,128]{3,2,1,0:T(8,128)(2,1)S(1)}, u32[]{:S(2)}, u32[]{:S(2)}) %all-to-all-start) | async-done | bytes 3145760 | tf_op jit(solution)/shard_map/all_to_all | solution.py:303
  77.1 0.0 copy-start
  77.1 1.7 copy-done
  78.8 86.5 %scores.1 = f32[96,192]{1,0:T(8,128)} custom-call(s32[12]{0:T(128)} %fusion.3.picks, bf16[48,256,128]{2,1,0:T(8,128)(2,1)} %bitcast.18, bf16[384,128]{1,0:T(8,128)(2,1)} %constant.51.clone.forward, bf16[256,256]{1,0:T(8,128)(2,1)} %constant.52.clone.swap, bf16[256,256]{1,0:T(8,128)(2,1)} %constant.53.clone.mirror, bf16[256,256]{1,0:T(8,128)(2,1)} %constant.54.clone.shift), custom_call_target="tpu_custom_call" | custom-call | tf_op jit(solution)/shard_map/scores/pallas_call | solution.py:267
  165.3 1.5 copy.15
  (6 shorter events, 0.0 us)
Async XLA Ops:
  28.7 48.4 %all-to-all-start = ((bf16[16,3,256,128]{3,2,1,0:T(8,128)(2,1)}), bf16[16,3,256,128]{3,2,1,0:T(8,128)(2,1)S(1)}, u32[]{:S(2)}, u32[]{:S(2)}) async-start(bf16[16,3,256,128]{3,2,1,0:T(8,128)(2,1)} %bitcast.19), calls=%async_computation | async-start | bytes 6291456 | tf_op jit(solution)/shard_map/all_to_all | solution.py:303
  77.1 1.7 copy-start
where the time goes:
time: 167 us
  Pallas kernels  86.5 us (52%)
  waiting for transfers between devices  41 us (25%)
  local copies, waits for them, and re-layouts  17.8 us (11%)
  blocking collectives  11.2 us (7%)
  starting transfers between devices  6.62 us (4%)
  other arithmetic  3.04 us (2%)
    pallas_call x1, Pallas kernels, scores_of(): pl.pallas_call(score_kernel, out_shape=jax.ShapeDtypeStruct((COLS * M, RO...  86.5 us
    all_to_all x1, waiting for transfers between devices, body(): lax.all_to_all(payload, 'row', split_axis=0, concat_axis=0, tiled=True)  41 us
    unnamed x8, local copies, waits for them, and re-layouts  13.4 us
    broadcast_in_dim x1, blocking collectives, body(): jnp.where(source_ids[None, :] < source_ids[:, None], shard_counts[None, :...  11.2 us
    all_to_all x1, starting transfers between devices, body(): lax.all_to_all(payload, 'row', split_axis=0, concat_axis=0, tiled=True)  6.62 us
    gather x1, local copies, waits for them, and re-layouts, body(): crossings.reshape(slot_total, -1)[chosen]  4.26 us
  transfers between devices with their start and end apart: 1, of which 1 were waited for; matrix products, arithmetic and copies ran while one was open for 0% of the time, Pallas kernels for 0%

commit v1 on v0

--- a/solution.py
+++ b/solution.py
@@ -76,10 +76,19 @@
     return r // 8, (r // 2) % 4, r % 2, c // 2, c % 2
 
 
+OTHERS = [
+    (1, 2, 0), (1, 2, 1), (0, 2, 0), (0, 2, 1), (1, 1, 0), (1, 3, 0), (1, 1, 1), (1, 3, 1),
+    (0, 1, 0), (0, 3, 0), (0, 1, 1), (0, 3, 1), (1, 0, 0), (1, 0, 1), (0, 0, 1),
+]
+
+
 def score_kernel(
-    picks, planes, forward, swap, mirror, shift, out,
-    cols, leads, y_lead, y_col, gram_a, gram_b, e_lead, e_col, send, recv,
+    count, slots, crossings, forward, swap, mirror, shift, out,
+    held, staged, planes, tallies, tally, picks, cols, leads, y_lead, y_col, gram_a, gram_b, e_lead, e_col,
+    load, tally_sem, send, recv, hand_out, hand_in, count_out, count_in,
 ):
+    fetch = pltpu.make_async_copy(crossings, held, load)
+    fetch.start()
     z, x, k, y, h = place()
     my_row = z * 8 + x * 2 + k
     my_col = y * 2 + h
@@ -95,18 +104,79 @@
     zh, yp, ym = (my_row, col_at(1, 0)), (my_row, col_at(0, 1)), (my_row, col_at(0, 3))
 
     barrier = pltpu.get_barrier_semaphore()
-    for device in (sib, zl, xp, xm, zh, yp, ym):
+    others = [(row_at(*step), my_col) for step in OTHERS]
+    for device in others + [zh, yp, ym]:
         pl.semaphore_signal(barrier, inc=1, device_id=device, device_id_type=MESH)
-    pl.semaphore_wait(barrier, 7)
-
-    def transform(p, _):
-        parts = dot_nt(forward[...], planes[picks[p]])
-        value = (parts[:NX] + (parts[NX : 2 * NX] + parts[2 * NX :])).astype(bf16)
-        cols[my_row, p] = value
-        leads[my_col, p] = value
-        return 0
-
-    lax.fori_loop(0, M, transform, 0)
+    tallies[my_row] = jnp.full((8, 128), count[0, 0], jnp.int32)
+    pl.semaphore_wait(barrier, len(OTHERS) + 3)
+
+    def tell(e, row, device):
+        return pltpu.make_async_remote_copy(
+            src_ref=tallies.at[row],
+            dst_ref=tallies.at[row],
+            send_sem=count_out.at[e],
+            recv_sem=count_in.at[e],
+            device_id=device,
+            device_id_type=MESH,
+        )
+
+    def hand(e, row, source, device):
+        return pltpu.make_async_remote_copy(
+            src_ref=staged.at[row],
+            dst_ref=planes.at[source],
+            send_sem=hand_out.at[e],
+            recv_sem=hand_in.at[e],
+            device_id=device,
+            device_id_type=MESH,
+        )
+
+    senders = [row_at(dz, -dx, dk) for dz, dx, dk in OTHERS]
+    for e, device in enumerate(others):
+        tell(e, my_row, device).start()
+    for e, device in enumerate(others):
+        tell(e, senders[e], device).wait_recv()
+    to_scalar = pltpu.make_async_copy(tallies, tally, tally_sem)
+    to_scalar.start()
+    fetch.wait()
+    to_scalar.wait()
+    my_offset = jnp.int32(0)
+    for r in range(ROWS):
+        my_offset = my_offset + jnp.where(r < my_row, tally[r, 0, 0], 0)
+
+    for e, device in enumerate(others):
+        target = device[0]
+        for t in range(BUCKETS):
+            staged[target, t] = held[slots[t * ROWS + (target + 256 * ROWS - my_offset) % ROWS]]
+        hand(e, target, my_row, device).start()
+    for t in range(BUCKETS):
+        planes[my_row, t] = held[slots[t * ROWS + (my_row + 256 * ROWS - my_offset) % ROWS]]
+
+    def pick(p, _):
+        wanted = p * ROWS + my_row
+        offset, found = jnp.int32(0), jnp.int32(0)
+        for r in range(ROWS):
+            within = wanted - offset
+            hit = (within >= 0) & (within < tally[r, 0, 0])
+            found = jnp.where(hit, r * BUCKETS + within // ROWS, found)
+            offset = offset + tally[r, 0, 0]
+        picks[p] = found
+        return 0
+
+    lax.fori_loop(0, M, pick, 0)
+    for e, device in enumerate(others):
+        hand(e, others[e][0], senders[e], device).wait_recv()
+
+    def transform(b, _):
+        for u in range(3):
+            p = b * 3 + u
+            source = picks[p]
+            parts = dot_nt(forward[...], planes[source // BUCKETS, source % BUCKETS])
+            value = (parts[:NX] + (parts[NX : 2 * NX] + parts[2 * NX :])).astype(bf16)
+            cols[my_row, p] = value
+            leads[my_col, p] = value
+        return 0
+
+    lax.fori_loop(0, M // 3, transform, 0)
 
     def piece(ref, slot, t):
         return ref.at[slot, :, pl.ds(pl.multiple_of(t * 16, 16), 16), :]
@@ -260,16 +330,26 @@
         return 0
 
     lax.fori_loop(0, PARTS, finish, 0)
-
-
-def scores_of(picks, planes):
+    for e, device in enumerate(others):
+        tell(e, my_row, device).wait_send()
+        hand(e, device[0], my_row, device).wait_send()
+
+
+def scores_of(count, slots, crossings):
     vmem = pl.BlockSpec(memory_space=pltpu.VMEM)
+    smem = pl.BlockSpec(memory_space=pltpu.SMEM)
     return pl.pallas_call(
         score_kernel,
         out_shape=jax.ShapeDtypeStruct((COLS * M, ROWS * M), f32),
-        in_specs=[pl.BlockSpec(memory_space=pltpu.SMEM)] + [vmem] * 5,
+        in_specs=[smem, smem, pl.BlockSpec(memory_space=pl.ANY)] + [vmem] * 4,
         out_specs=vmem,
         scratch_shapes=[
+            pltpu.VMEM((BUCKETS * ROWS, ENTRIES, NX), bf16),
+            pltpu.VMEM((ROWS, BUCKETS, ENTRIES, NX), bf16),
+            pltpu.VMEM((ROWS, BUCKETS, ENTRIES, NX), bf16),
+            pltpu.VMEM((ROWS, 8, 128), jnp.int32),
+            pltpu.SMEM((ROWS, 8, 128), jnp.int32),
+            pltpu.SMEM((M,), jnp.int32),
             pltpu.VMEM((ROWS, M, NX, ENTRIES), bf16),
             pltpu.VMEM((COLS, M, NX, ENTRIES), bf16),
             pltpu.VMEM((16, 192, ENTRIES), bf16),
@@ -278,34 +358,27 @@
             pltpu.VMEM((NX * PITCH, 128), f32),
             pltpu.VMEM((96, 128), f32),
             pltpu.VMEM((192, 128), f32),
+            pltpu.SemaphoreType.DMA,
+            pltpu.SemaphoreType.DMA,
             pltpu.SemaphoreType.DMA((22, PARTS)),
             pltpu.SemaphoreType.DMA((22, PARTS)),
+            pltpu.SemaphoreType.DMA((15,)),
+            pltpu.SemaphoreType.DMA((15,)),
+            pltpu.SemaphoreType.DMA((15,)),
+            pltpu.SemaphoreType.DMA((15,)),
         ],
         compiler_params=pltpu.CompilerParams(
             collective_id=1, has_side_effects=True, vmem_limit_bytes=60 * 2**20
         ),
         name="scores",
-    )(picks, planes, *[jnp.asarray(table) for table in tables()])
+    )(count, slots, crossings, *[jnp.asarray(table) for table in tables()])
 
 
 def body(crossings, counts, dest):
-    my_row = lax.axis_index("row")
     slot_total = crossings.shape[0]
-    shard_counts = lax.all_gather(counts, "row", axis=1, tiled=True).reshape(ROWS)
-    source_ids = jnp.arange(ROWS, dtype=jnp.int32)
-    offsets = jnp.sum(jnp.where(source_ids[None, :] < source_ids[:, None], shard_counts[None, :], 0), 1)
-    my_offset = jnp.sum(jnp.where(source_ids < my_row, shard_counts, 0))
     slot_ids = jnp.arange(slot_total, dtype=jnp.int32)
-    buckets = jnp.arange(BUCKETS, dtype=jnp.int32)[None, :]
-    outgoing = (buckets * ROWS + (source_ids[:, None] - my_offset) % ROWS).reshape(-1)
-    chosen = jnp.sum(jnp.where(dest.reshape(1, -1) == outgoing[:, None], slot_ids[None, :], 0), 1)
-    payload = crossings.reshape(slot_total, -1)[chosen].reshape(ROWS, BUCKETS, ENTRIES, NX)
-    received = lax.all_to_all(payload, "row", split_axis=0, concat_axis=0, tiled=True)
-    wanted = jnp.arange(M, dtype=jnp.int32)[:, None] * ROWS + my_row
-    within = wanted - offsets[None, :]
-    hit = (within >= 0) & (within < shard_counts[None, :])
-    picks = jnp.sum(jnp.where(hit, source_ids[None, :] * BUCKETS + within // ROWS, 0), 1)
-    return scores_of(picks, received.reshape(slot_total, ENTRIES, NX))
+    slots = jnp.sum(jnp.where(dest.reshape(1, -1) == slot_ids[:, None], slot_ids[None, :], 0), 1)
+    return scores_of(counts, slots, crossings.reshape(slot_total, ENTRIES, NX))
 
 
 def solution(mesh):

time: 167 us -> 140 us (0.84)
  Pallas kernels: 86.5 us -> 136 us
  waiting for transfers between devices: 41 us -> 0 us
  local copies, waits for them, and re-layouts: 17.8 us -> 1.54 us
  blocking collectives: 11.2 us -> 0 us
  starting transfers between devices: 6.62 us -> 0 us
  other arithmetic: 3.04 us -> 1.28 us
    pallas_call x1, Pallas kernels: 86.5 us -> 136 us  [scores_of(): pl.pallas_call(score_kernel, out_shape=jax.ShapeDtypeStruct((COLS * M, RO...]
    all_to_all x1 -> x0, waiting for transfers between devices: 41 us -> none  [body(): lax.all_to_all(payload, 'row', split_axis=0, concat_axis=0, tiled=True)]
    unnamed x8 -> x1, local copies, waits for them, and re-layouts: 13.4 us -> 1.54 us
    broadcast_in_dim x1 -> x0, blocking collectives: 11.2 us -> none  [body(): jnp.where(source_ids[None, :] < source_ids[:, None], shard_counts[None, :...]
    all_to_all x1 -> x0, starting transfers between devices: 6.62 us -> none  [body(): lax.all_to_all(payload, 'row', split_axis=0, concat_axis=0, tiled=True)]
    gather x1 -> x0, local copies, waits for them, and re-layouts: 4.26 us -> none  [body(): crossings.reshape(slot_total, -1)[chosen]]
  transfers between devices with their start and end apart: 1 -> 0, of which waited for: 1 -> 0; matrix products, arithmetic and copies ran while one was open for 0% -> 0% of each run, Pallas kernels for 0% -> 0%
where the time goes in v1:
time: 140 us
  Pallas kernels  136 us (97%)
  local copies, waits for them, and re-layouts  1.54 us (1%)
    pallas_call x1, Pallas kernels, scores_of(): pl.pallas_call(score_kernel, out_shape=jax.ShapeDtypeStruct((COLS * M, RO...  136 us

profile of v1, /device:TPU:1, one launch (start us, length us, event | category | flops | bytes accessed | tf_op | source)
XLA Modules:
  0.0 139.9 jit_solution(6720024267260844009)
XLA Ops:
  0.7 1.3 select_reduce_fusion.slots
  1.9 136.4 %scores.1 = f32[96,192]{1,0:T(8,128)} custom-call(s32[1,1]{1,0:T(1,128)S(6)} %copy.9.count, s32[48]{0:T(128)} %select_reduce_fusion.slots, bf16[48,256,128]{2,1,0:T(8,128)(2,1)} %bitcast.2, bf16[384,128]{1,0:T(8,128)(2,1)} %constant.10.clone.forward, bf16[256,256]{1,0:T(8,128)(2,1)} %constant.11.clone.swap, bf16[256,256]{1,0:T(8,128)(2,1)} %constant.12.clone.mirror, ...), custom_call_target="tpu_custom_call" | custom-call | tf_op jit(solution)/shard_map/scores/pallas_call | solution.py:341
  138.3 1.5 %copy.10 = f32[96,192]{1,0:T(8,128)} copy(f32[96,192]{1,0:T(8,128)} %scores.1) | data formatting | bytes 147456

commit v2 on v1

--- a/solution.py
+++ b/solution.py
@@ -16,7 +16,9 @@
 COLS = 8
 BUCKETS = 3
 PARTS = 8
-PITCH = 200
+PITCH_A = 200
+PITCH_B = 104
+AHEAD = 2
 
 epsilon = 1e-06
 
@@ -77,15 +79,15 @@
 
 
 OTHERS = [
-    (1, 2, 0), (1, 2, 1), (0, 2, 0), (0, 2, 1), (1, 1, 0), (1, 3, 0), (1, 1, 1), (1, 3, 1),
-    (0, 1, 0), (0, 3, 0), (0, 1, 1), (0, 3, 1), (1, 0, 0), (1, 0, 1), (0, 0, 1),
+    (1, 2, 0), (0, 1, 0), (0, 3, 0), (1, 0, 0), (0, 2, 0), (1, 1, 1), (1, 3, 1), (1, 2, 1), (0, 1, 1), (0, 3, 1),
+    (1, 0, 1), (0, 2, 1), (1, 1, 0), (1, 3, 0), (0, 0, 1),
 ]
 
 
 def score_kernel(
-    count, slots, crossings, forward, swap, mirror, shift, out,
-    held, staged, planes, tallies, tally, picks, cols, leads, y_lead, y_col, gram_a, gram_b, e_lead, e_col,
-    load, tally_sem, send, recv, hand_out, hand_in, count_out, count_in,
+    count, dest, crossings, forward, swap, mirror, shift, out,
+    held, staged, planes, tally, slots, picks, cols, leads, y_lead, y_col, gram_a, gram_b, e_lead, e_col,
+    load, send, recv, hand_out, hand_in, count_out, count_in,
 ):
     fetch = pltpu.make_async_copy(crossings, held, load)
     fetch.start()
@@ -107,13 +109,13 @@
     others = [(row_at(*step), my_col) for step in OTHERS]
     for device in others + [zh, yp, ym]:
         pl.semaphore_signal(barrier, inc=1, device_id=device, device_id_type=MESH)
-    tallies[my_row] = jnp.full((8, 128), count[0, 0], jnp.int32)
+    tally[my_row, 0] = count[0, 0]
     pl.semaphore_wait(barrier, len(OTHERS) + 3)
 
     def tell(e, row, device):
         return pltpu.make_async_remote_copy(
-            src_ref=tallies.at[row],
-            dst_ref=tallies.at[row],
+            src_ref=tally.at[row],
+            dst_ref=tally.at[row],
             send_sem=count_out.at[e],
             recv_sem=count_in.at[e],
             device_id=device,
@@ -133,15 +135,21 @@
     senders = [row_at(dz, -dx, dk) for dz, dx, dk in OTHERS]
     for e, device in enumerate(others):
         tell(e, my_row, device).start()
+
+    def find(n, _):
+        slot = jnp.int32(0)
+        for s in range(BUCKETS * ROWS):
+            slot = jnp.where(dest[0, s] == n, s, slot)
+        slots[n] = slot
+        return 0
+
+    lax.fori_loop(0, BUCKETS * ROWS, find, 0)
     for e, device in enumerate(others):
         tell(e, senders[e], device).wait_recv()
-    to_scalar = pltpu.make_async_copy(tallies, tally, tally_sem)
-    to_scalar.start()
     fetch.wait()
-    to_scalar.wait()
     my_offset = jnp.int32(0)
     for r in range(ROWS):
-        my_offset = my_offset + jnp.where(r < my_row, tally[r, 0, 0], 0)
+        my_offset = my_offset + jnp.where(r < my_row, tally[r, 0], 0)
 
     for e, device in enumerate(others):
         target = device[0]
@@ -156,9 +164,9 @@
         offset, found = jnp.int32(0), jnp.int32(0)
         for r in range(ROWS):
             within = wanted - offset
-            hit = (within >= 0) & (within < tally[r, 0, 0])
+            hit = (within >= 0) & (within < tally[r, 0])
             found = jnp.where(hit, r * BUCKETS + within // ROWS, found)
-            offset = offset + tally[r, 0, 0]
+            offset = offset + tally[r, 0]
         picks[p] = found
         return 0
 
@@ -172,14 +180,15 @@
             source = picks[p]
             parts = dot_nt(forward[...], planes[source // BUCKETS, source % BUCKETS])
             value = (parts[:NX] + (parts[NX : 2 * NX] + parts[2 * NX :])).astype(bf16)
-            cols[my_row, p] = value
-            leads[my_col, p] = value
+            for t in range(PARTS):
+                cols[my_row, t, p] = value[t * 16 : (t + 1) * 16]
+                leads[my_col, t, p] = value[t * 16 : (t + 1) * 16]
         return 0
 
     lax.fori_loop(0, M // 3, transform, 0)
 
     def piece(ref, slot, t):
-        return ref.at[slot, :, pl.ds(pl.multiple_of(t * 16, 16), 16), :]
+        return ref.at[slot, t]
 
     def copy(flow, ref, slot, t, device):
         block = piece(ref, slot, t)
@@ -226,13 +235,11 @@
     e_col[...] = jnp.zeros_like(e_col)
 
     def score_part(t):
-        r0 = pl.ds(pl.multiple_of(t * 16, 16), 16)
         order = swap[...]
 
         def relay(ref, groups, dst):
-            flat = ref.reshape(groups * 16, NX, ENTRIES)
             for g in range(groups):
-                block = flat[g * 16 : (g + 1) * 16, r0, :].reshape(256, ENTRIES)
+                block = jnp.concatenate([ref[b // M, t, b % M] for b in range(g * 16, (g + 1) * 16)], 0)
                 turned = jnp.dot(order, block, preferred_element_type=f32).astype(bf16)
                 dst[:, g * 16 : (g + 1) * 16, :] = turned.reshape(16, 16, ENTRIES)
 
@@ -260,40 +267,48 @@
             else:
                 real, imag = rr + ii, ri - ir
             for value, j in ((real, i), (imag, 8 + i)):
-                base = pl.ds(pl.multiple_of((t * 16 + j) * PITCH, 8), 192)
-                gram_a[base, :] = value[:, :128]
-                gram_b[base, :64] = value[:, 128:]
+                gram_a[pl.ds(pl.multiple_of((t * 16 + j) * PITCH_A, 8), 192), :] = value[:, :128]
+                pair = jnp.concatenate([value[:96, 128:], value[96:, 128:]], 1)
+                gram_b[pl.ds(pl.multiple_of((t * 16 + j) * PITCH_B, 8), 96), :] = pair
+
+    own = (0, 15, 1, 3, 16, 18, 7)
+    for t in range(AHEAD):
+        start(own, t)
 
     def step(s, _):
+        @pl.when(s < PARTS - AHEAD)
+        def _():
+            start(own, s + AHEAD)
+
         @pl.when(s < PARTS)
         def _():
-            start((0, 1, 3, 15, 16, 18, 7), s)
+            wait_in((0, 15), s)
+            start((2, 4, 17, 19, 8), s)
 
         @pl.when((s >= 1) & (s < PARTS + 1))
         def _():
-            wait_in((0, 15), s - 1)
-            start((2, 4, 17, 19, 8), s - 1)
+            wait_in((1, 16), s - 1)
+            start((5, 20, 9), s - 1)
+            wait_in((4, 19), s - 1)
+            start((6, 21, 12), s - 1)
+            wait_in((2, 3), s - 1)
+            start((10, 11), s - 1)
 
         @pl.when((s >= 2) & (s < PARTS + 2))
         def _():
-            wait_in((1, 4, 16, 19), s - 2)
-            start((5, 6, 20, 21, 9, 12), s - 2)
-            wait_in((2, 3), s - 2)
-            start((10, 11), s - 2)
-
-        @pl.when((s >= 3) & (s < PARTS + 3))
+            wait_in((5, 6), s - 2)
+            start((13, 14), s - 2)
+
+        @pl.when(s >= 3)
         def _():
-            wait_in((5, 6), s - 3)
-            start((13, 14), s - 3)
-
-        @pl.when(s >= 4)
-        def _():
-            wait_in((17, 18, 20, 21, 7, 8, 9, 10, 11, 12, 13, 14), s - 4)
-            score_part(s - 4)
+            wait_in((17, 18, 20, 21, 7, 8, 9, 10, 11, 12, 13, 14), s - 3)
+            score_part(s - 3)
+            for flow, (ref, slot, device) in sends.items():
+                copy(flow, ref, slot, s - 3, device).wait_send()
 
         return 0
 
-    lax.fori_loop(0, PARTS + 4, step, 0)
+    lax.fori_loop(0, PARTS + 3, step, 0)
 
     scale_lead = jnp.sqrt(jnp.sum(e_lead[...], -1, keepdims=True) / (NX * NX * ENTRIES) + epsilon)
     ones = jnp.ones((8, 128), f32)
@@ -304,38 +319,36 @@
 
     def best(b, _):
         found = []
-        for u in range(8):
-            a = b * 8 + u
+        for u in range(0, 8, 2):
             values = []
-            for start_row in (a, a + 96):
-                values.append(gram_a[pl.ds(start_row, NX, stride=PITCH), :])
-                values.append(gram_b[pl.ds(start_row, NX, stride=PITCH), :][:, :64])
+            for a in (b * 8 + u, b * 8 + u + 1):
+                values.append(gram_a[pl.ds(a, NX, stride=PITCH_A), :])
+                values.append(gram_a[pl.ds(a + 96, NX, stride=PITCH_A), :])
+                values.append(gram_b[pl.ds(a, NX, stride=PITCH_B), :])
             value = jnp.concatenate(values, 1)
             high = value.astype(bf16)
             low = (value - high.astype(f32)).astype(bf16)
             moved = jnp.dot(to_shift, jnp.concatenate([high, low], 0), preferred_element_type=f32)
             top = jnp.max(moved[:NX] + moved[NX:], axis=0, keepdims=True)
-            found.append(jnp.maximum(top[:, :192], top[:, 192:]))
+            found.extend([top[:, :384], top[:, 384:]])
+        found = jnp.concatenate(found, 0)
+        found = jnp.concatenate(
+            [jnp.maximum(found[:, :128], found[:, 128:256]), jnp.maximum(found[:, 256:320], found[:, 320:])], 1
+        )
         rows = pl.ds(pl.multiple_of(b * 8, 8), 8)
         scale = e_lead[rows, :]
         scale = jnp.concatenate([scale, scale[:, :64]], 1)
-        out[rows, :] = jnp.concatenate(found, 0) / (math.sqrt(NX * ENTRIES) * scale * scale_col)
+        out[rows, :] = found / (math.sqrt(NX * ENTRIES) * scale * scale_col)
         return 0
 
     lax.fori_loop(0, 96 // 8, best, 0)
 
-    def finish(t, _):
-        for flow, (ref, slot, device) in sends.items():
-            copy(flow, ref, slot, t, device).wait_send()
-        return 0
-
-    lax.fori_loop(0, PARTS, finish, 0)
     for e, device in enumerate(others):
         tell(e, my_row, device).wait_send()
         hand(e, device[0], my_row, device).wait_send()
 
 
-def scores_of(count, slots, crossings):
+def scores_of(count, dest, crossings):
     vmem = pl.BlockSpec(memory_space=pltpu.VMEM)
     smem = pl.BlockSpec(memory_space=pltpu.SMEM)
     return pl.pallas_call(
@@ -347,18 +360,17 @@
             pltpu.VMEM((BUCKETS * ROWS, ENTRIES, NX), bf16),
             pltpu.VMEM((ROWS, BUCKETS, ENTRIES, NX), bf16),
             pltpu.VMEM((ROWS, BUCKETS, ENTRIES, NX), bf16),
-            pltpu.VMEM((ROWS, 8, 128), jnp.int32),
-            pltpu.SMEM((ROWS, 8, 128), jnp.int32),
+            pltpu.SMEM((ROWS, 128), jnp.int32),
+            pltpu.SMEM((BUCKETS * ROWS,), jnp.int32),
             pltpu.SMEM((M,), jnp.int32),
-            pltpu.VMEM((ROWS, M, NX, ENTRIES), bf16),
-            pltpu.VMEM((COLS, M, NX, ENTRIES), bf16),
+            pltpu.VMEM((ROWS, PARTS, M, 16, ENTRIES), bf16),
+            pltpu.VMEM((COLS, PARTS, M, 16, ENTRIES), bf16),
             pltpu.VMEM((16, 192, ENTRIES), bf16),
             pltpu.VMEM((16, 192, ENTRIES), bf16),
-            pltpu.VMEM((NX * PITCH, 128), f32),
-            pltpu.VMEM((NX * PITCH, 128), f32),
+            pltpu.VMEM((NX * PITCH_A, 128), f32),
+            pltpu.VMEM((NX * PITCH_B, 128), f32),
             pltpu.VMEM((96, 128), f32),
             pltpu.VMEM((192, 128), f32),
-            pltpu.SemaphoreType.DMA,
             pltpu.SemaphoreType.DMA,
             pltpu.SemaphoreType.DMA((22, PARTS)),
             pltpu.SemaphoreType.DMA((22, PARTS)),
@@ -371,14 +383,11 @@
             collective_id=1, has_side_effects=True, vmem_limit_bytes=60 * 2**20
         ),
         name="scores",
-    )(count, slots, crossings, *[jnp.asarray(table) for table in tables()])
+    )(count, dest, crossings, *[jnp.asarray(table) for table in tables()])
 
 
 def body(crossings, counts, dest):
-    slot_total = crossings.shape[0]
-    slot_ids = jnp.arange(slot_total, dtype=jnp.int32)
-    slots = jnp.sum(jnp.where(dest.reshape(1, -1) == slot_ids[:, None], slot_ids[None, :], 0), 1)
-    return scores_of(counts, slots, crossings.reshape(slot_total, ENTRIES, NX))
+    return scores_of(counts, dest, crossings.reshape(BUCKETS * ROWS, ENTRIES, NX))
 
 
 def solution(mesh):

time: 140 us -> 130 us (0.929)
  Pallas kernels: 136 us -> 128 us
    pallas_call x1, Pallas kernels: 136 us -> 128 us  [scores_of(): pl.pallas_call(score_kernel, out_shape=jax.ShapeDtypeStruct((COLS * M, RO...]
where the time goes in v2:
time: 130 us
  Pallas kernels  128 us (98%)
  local copies, waits for them, and re-layouts  1.54 us (1%)
    pallas_call x1, Pallas kernels, scores_of(): pl.pallas_call(score_kernel, out_shape=jax.ShapeDtypeStruct((COLS * M, RO...  128 us

profile of v2, /device:TPU:1, one launch (start us, length us, event | category | flops | bytes accessed | tf_op | source)
XLA Modules:
  0.0 129.9 jit_solution(9472915623406159129)
XLA Ops:
  0.7 127.7 %scores.1 = f32[96,192]{1,0:T(8,128)} custom-call(s32[1,1]{1,0:T(1,128)S(6)} %copy.9.count, s32[1,48]{1,0:T(1,128)} %dest.1, bf16[48,256,128]{2,1,0:T(8,128)(2,1)} %bitcast.1, bf16[384,128]{1,0:T(8,128)(2,1)} %constant.8.clone.forward, bf16[256,256]{1,0:T(8,128)(2,1)} %constant.9.clone.swap, bf16[256,256]{1,0:T(8,128)(2,1)} %constant.10.clone.mirror, ...), custom_call_target="tpu_custom_call" | custom-call | tf_op jit(solution)/shard_map/scores/pallas_call | solution.py:354
  128.4 1.5 %copy.10 = f32[96,192]{1,0:T(8,128)} copy(f32[96,192]{1,0:T(8,128)} %scores.1) | data formatting | bytes 147456

commit v3 on v2

--- a/solution.py
+++ b/solution.py
@@ -18,7 +18,10 @@
 PARTS = 8
 PITCH_A = 200
 PITCH_B = 104
-AHEAD = 2
+GROUP = 2
+GROUPS = PARTS // GROUP
+EARLY = 2
+AHEAD = 3
 
 epsilon = 1e-06
 
@@ -86,7 +89,7 @@
 
 def score_kernel(
     count, dest, crossings, forward, swap, mirror, shift, out,
-    held, staged, planes, tally, slots, picks, cols, leads, y_lead, y_col, gram_a, gram_b, e_lead, e_col,
+    held, coeffs, staged, planes_0, planes_1, planes_2, planes_3, tally, slots, picks, cols, leads, y_lead, y_col, gram_a, gram_b, e_lead, e_col,
     load, send, recv, hand_out, hand_in, count_out, count_in,
 ):
     fetch = pltpu.make_async_copy(crossings, held, load)
@@ -122,12 +125,14 @@
             device_id_type=MESH,
         )
 
-    def hand(e, row, source, device):
+    planes = (planes_0, planes_1, planes_2, planes_3)
+
+    def hand(e, group, row, source, device):
         return pltpu.make_async_remote_copy(
-            src_ref=staged.at[row],
-            dst_ref=planes.at[source],
-            send_sem=hand_out.at[e],
-            recv_sem=hand_in.at[e],
+            src_ref=staged.at[row, group],
+            dst_ref=planes[group].at[source],
+            send_sem=hand_out.at[e, group],
+            recv_sem=hand_in.at[e, group],
             device_id=device,
             device_id_type=MESH,
         )
@@ -135,29 +140,53 @@
     senders = [row_at(dz, -dx, dk) for dz, dx, dk in OTHERS]
     for e, device in enumerate(others):
         tell(e, my_row, device).start()
-
-    def find(n, _):
-        slot = jnp.int32(0)
-        for s in range(BUCKETS * ROWS):
-            slot = jnp.where(dest[0, s] == n, s, slot)
-        slots[n] = slot
+    fetch.wait()
+
+    def prepare(b, _):
+        for u in range(4):
+            n = b * 4 + u
+            slot = jnp.int32(0)
+            for s in range(BUCKETS * ROWS):
+                slot = jnp.where(dest[0, s] == n, s, slot)
+            slots[n] = slot
+            parts = dot_nt(forward[...], held[n])
+            value = (parts[:NX] + (parts[NX : 2 * NX] + parts[2 * NX :])).astype(bf16)
+            for t in range(PARTS):
+                coeffs[n, t] = value[t * 16 : (t + 1) * 16]
         return 0
 
-    lax.fori_loop(0, BUCKETS * ROWS, find, 0)
+    lax.fori_loop(0, BUCKETS * ROWS // 4, prepare, 0)
     for e, device in enumerate(others):
         tell(e, senders[e], device).wait_recv()
-    fetch.wait()
     my_offset = jnp.int32(0)
     for r in range(ROWS):
         my_offset = my_offset + jnp.where(r < my_row, tally[r, 0], 0)
 
-    for e, device in enumerate(others):
-        target = device[0]
+    def hand_over(group):
+        for e, device in enumerate(others):
+            target = device[0]
+            for t in range(BUCKETS):
+                slot = slots[t * ROWS + (target + 256 * ROWS - my_offset) % ROWS]
+                for g in range(GROUP):
+                    staged[target, group, t, g] = coeffs[slot, group * GROUP + g]
+            hand(e, group, target, my_row, device).start()
         for t in range(BUCKETS):
-            staged[target, t] = held[slots[t * ROWS + (target + 256 * ROWS - my_offset) % ROWS]]
-        hand(e, target, my_row, device).start()
-    for t in range(BUCKETS):
-        planes[my_row, t] = held[slots[t * ROWS + (my_row + 256 * ROWS - my_offset) % ROWS]]
+            slot = slots[t * ROWS + (my_row + 256 * ROWS - my_offset) % ROWS]
+            for g in range(GROUP):
+                planes[group][my_row, t, g] = coeffs[slot, group * GROUP + g]
+
+    def take(group):
+        for e, device in enumerate(others):
+            hand(e, group, device[0], senders[e], device).wait_recv()
+        for p in range(M):
+            source = picks[p]
+            for g in range(GROUP):
+                value = planes[group][source // BUCKETS, source % BUCKETS, g]
+                cols[my_row, group * GROUP + g, p] = value
+                leads[my_col, group * GROUP + g, p] = value
+
+    for group in range(EARLY):
+        hand_over(group)
 
     def pick(p, _):
         wanted = p * ROWS + my_row
@@ -171,21 +200,6 @@
         return 0
 
     lax.fori_loop(0, M, pick, 0)
-    for e, device in enumerate(others):
-        hand(e, others[e][0], senders[e], device).wait_recv()
-
-    def transform(b, _):
-        for u in range(3):
-            p = b * 3 + u
-            source = picks[p]
-            parts = dot_nt(forward[...], planes[source // BUCKETS, source % BUCKETS])
-            value = (parts[:NX] + (parts[NX : 2 * NX] + parts[2 * NX :])).astype(bf16)
-            for t in range(PARTS):
-                cols[my_row, t, p] = value[t * 16 : (t + 1) * 16]
-                leads[my_col, t, p] = value[t * 16 : (t + 1) * 16]
-        return 0
-
-    lax.fori_loop(0, M // 3, transform, 0)
 
     def piece(ref, slot, t):
         return ref.at[slot, t]
@@ -271,44 +285,49 @@
                 pair = jnp.concatenate([value[:96, 128:], value[96:, 128:]], 1)
                 gram_b[pl.ds(pl.multiple_of((t * 16 + j) * PITCH_B, 8), 96), :] = pair
 
-    own = (0, 15, 1, 3, 16, 18, 7)
-    for t in range(AHEAD):
-        start(own, t)
-
     def step(s, _):
-        @pl.when(s < PARTS - AHEAD)
-        def _():
-            start(own, s + AHEAD)
+        for group in range(GROUPS):
+            @pl.when(s == group * GROUP)
+            def _():
+                take(group)
+                if group + EARLY < GROUPS:
+                    hand_over(group + EARLY)
 
         @pl.when(s < PARTS)
         def _():
-            wait_in((0, 15), s)
-            start((2, 4, 17, 19, 8), s)
-
-        @pl.when((s >= 1) & (s < PARTS + 1))
+            start((0, 15, 1, 3, 16, 18, 7), s)
+
+        @pl.when((s >= AHEAD) & (s < PARTS + AHEAD))
         def _():
-            wait_in((1, 16), s - 1)
-            start((5, 20, 9), s - 1)
-            wait_in((4, 19), s - 1)
-            start((6, 21, 12), s - 1)
-            wait_in((2, 3), s - 1)
-            start((10, 11), s - 1)
-
-        @pl.when((s >= 2) & (s < PARTS + 2))
+            wait_in((0, 15), s - AHEAD)
+            start((2, 4, 17, 19, 8), s - AHEAD)
+
+        @pl.when((s >= AHEAD + 1) & (s < PARTS + AHEAD + 1))
         def _():
-            wait_in((5, 6), s - 2)
-            start((13, 14), s - 2)
-
-        @pl.when(s >= 3)
+            t = s - AHEAD - 1
+            wait_in((1, 16), t)
+            start((5, 20, 9), t)
+            wait_in((4, 19), t)
+            start((6, 21, 12), t)
+            wait_in((2, 3), t)
+            start((10, 11), t)
+
+        @pl.when((s >= AHEAD + 2) & (s < PARTS + AHEAD + 2))
         def _():
-            wait_in((17, 18, 20, 21, 7, 8, 9, 10, 11, 12, 13, 14), s - 3)
-            score_part(s - 3)
+            wait_in((5, 6), s - AHEAD - 2)
+            start((13, 14), s - AHEAD - 2)
+
+        @pl.when(s >= AHEAD + 3)
+        def _():
+            t = s - AHEAD - 3
+            wait_in((17, 18, 20, 21, 7, 8, 9, 10, 11, 12, 13, 14), t)
+            score_part(t)
             for flow, (ref, slot, device) in sends.items():
-                copy(flow, ref, slot, s - 3, device).wait_send()
+                copy(flow, ref, slot, t, device).wait_send()
 
         return 0
 
-    lax.fori_loop(0, PARTS + 3, step, 0)
+    lax.fori_loop(0, PARTS + AHEAD + 3, step, 0)
 
     scale_lead = jnp.sqrt(jnp.sum(e_lead[...], -1, keepdims=True) / (NX * NX * ENTRIES) + epsilon)
     ones = jnp.ones((8, 128), f32)
@@ -345,7 +364,8 @@
 
     for e, device in enumerate(others):
         tell(e, my_row, device).wait_send()
-        hand(e, device[0], my_row, device).wait_send()
+        for group in range(GROUPS):
+            hand(e, group, device[0], my_row, device).wait_send()
 
 
 def scores_of(count, dest, crossings):
@@ -358,8 +378,9 @@
         out_specs=vmem,
         scratch_shapes=[
             pltpu.VMEM((BUCKETS * ROWS, ENTRIES, NX), bf16),
-            pltpu.VMEM((ROWS, BUCKETS, ENTRIES, NX), bf16),
-            pltpu.VMEM((ROWS, BUCKETS, ENTRIES, NX), bf16),
+            pltpu.VMEM((BUCKETS * ROWS, PARTS, 16, ENTRIES), bf16),
+            pltpu.VMEM((ROWS, GROUPS, BUCKETS, GROUP, 16, ENTRIES), bf16),
+            *[pltpu.VMEM((ROWS, BUCKETS, GROUP, 16, ENTRIES), bf16)] * GROUPS,
             pltpu.SMEM((ROWS, 128), jnp.int32),
             pltpu.SMEM((BUCKETS * ROWS,), jnp.int32),
             pltpu.SMEM((M,), jnp.int32),
@@ -374,8 +395,8 @@
             pltpu.SemaphoreType.DMA,
             pltpu.SemaphoreType.DMA((22, PARTS)),
             pltpu.SemaphoreType.DMA((22, PARTS)),
-            pltpu.SemaphoreType.DMA((15,)),
-            pltpu.SemaphoreType.DMA((15,)),
+            pltpu.SemaphoreType.DMA((15, GROUPS)),
+            pltpu.SemaphoreType.DMA((15, GROUPS)),
             pltpu.SemaphoreType.DMA((15,)),
             pltpu.SemaphoreType.DMA((15,)),
         ],

time: 130 us -> 121 us (0.931)
  Pallas kernels: 128 us -> 118 us
    pallas_call x1, Pallas kernels: 128 us -> 118 us  [scores_of(): pl.pallas_call(score_kernel, out_shape=jax.ShapeDtypeStruct((COLS * M, RO...]
where the time goes in v3:
time: 121 us
  Pallas kernels  118 us (98%)
  local copies, waits for them, and re-layouts  1.54 us (1%)
    pallas_call x1, Pallas kernels, scores_of(): pl.pallas_call(score_kernel, out_shape=jax.ShapeDtypeStruct((COLS * M, RO...  118 us

profile of v3, /device:TPU:1, one launch (start us, length us, event | category | flops | bytes accessed | tf_op | source)
XLA Modules:
  0.0 120.7 jit_solution(15313659941455506234)
XLA Ops:
  0.7 118.5 %scores.1 = f32[96,192]{1,0:T(8,128)} custom-call(s32[1,1]{1,0:T(1,128)S(6)} %copy.9.count, s32[1,48]{1,0:T(1,128)} %dest.1, bf16[48,256,128]{2,1,0:T(8,128)(2,1)} %bitcast.1, bf16[384,128]{1,0:T(8,128)(2,1)} %constant.8.clone.forward, bf16[256,256]{1,0:T(8,128)(2,1)} %constant.9.clone.swap, bf16[256,256]{1,0:T(8,128)(2,1)} %constant.10.clone.mirror, ...), custom_call_target="tpu_custom_call" | custom-call | tf_op jit(solution)/shard_map/scores/pallas_call | solution.py:374
  119.1 1.5 %copy.10 = f32[96,192]{1,0:T(8,128)} copy(f32[96,192]{1,0:T(8,128)} %scores.1) | data formatting | bytes 147456

commit v4 on v3

--- a/solution.py
+++ b/solution.py
@@ -274,7 +274,9 @@
             y_lead[j, 96:, :] = jnp.dot(y_lead[j, :96, :], turn, preferred_element_type=f32).astype(bf16)
         for i in range(8):
             lr, li, tr, ti = y_lead[i], y_lead[8 + i], y_col[i], y_col[8 + i]
-            rr, ii, ri, ir = dot_nt(lr, tr), dot_nt(li, ti), dot_nt(lr, ti), dot_nt(li, tr)
+            both = jnp.concatenate([lr, li], 0)
+            with_real, with_imag = dot_nt(both, tr), dot_nt(both, ti)
+            rr, ir, ri, ii = with_real[:192], with_real[192:], with_imag[:192], with_imag[192:]
             if i == 0:
                 real = rr + (1.0 - first) * ii
                 imag = first * ii + (1.0 - first) * (ri - ir)
@@ -336,7 +338,7 @@
     e_lead[...] = jnp.broadcast_to(scale_lead, (96, 128))
     to_shift = shift[...]
 
-    def best(b, _):
+    def some(b):
         found = []
         for u in range(0, 8, 2):
             values = []
@@ -358,9 +360,13 @@
         scale = e_lead[rows, :]
         scale = jnp.concatenate([scale, scale[:, :64]], 1)
         out[rows, :] = found / (math.sqrt(NX * ENTRIES) * scale * scale_col)
+
+    def best(b, _):
+        for u in range(4):
+            some(b * 4 + u)
         return 0
 
-    lax.fori_loop(0, 96 // 8, best, 0)
+    lax.fori_loop(0, 96 // 32, best, 0)
 
     for e, device in enumerate(others):
         tell(e, my_row, device).wait_send()

time: 121 us -> 119 us (0.983)
  Pallas kernels: 118 us -> 116 us
    pallas_call x1, Pallas kernels: 118 us -> 116 us  [scores_of(): pl.pallas_call(score_kernel, out_shape=jax.ShapeDtypeStruct((COLS * M, RO...]
where the time goes in v4:
time: 119 us; the launch traced here: 118 us
  Pallas kernels  116 us (97%)
  local copies, waits for them, and re-layouts  1.54 us (1%)
    pallas_call x1, Pallas kernels, scores_of(): pl.pallas_call(score_kernel, out_shape=jax.ShapeDtypeStruct((COLS * M, RO...  116 us

profile of v4, /device:TPU:1, one launch (start us, length us, event | category | flops | bytes accessed | tf_op | source)
XLA Modules:
  0.0 118.4 jit_solution(1455036719746383994)
XLA Ops:
  0.7 116.2 %scores.1 = f32[96,192]{1,0:T(8,128)} custom-call(s32[1,1]{1,0:T(1,128)S(6)} %copy.9.count, s32[1,48]{1,0:T(1,128)} %dest.1, bf16[48,256,128]{2,1,0:T(8,128)(2,1)} %bitcast.1, bf16[384,128]{1,0:T(8,128)(2,1)} %constant.8.clone.forward, bf16[256,256]{1,0:T(8,128)(2,1)} %constant.9.clone.swap, bf16[256,256]{1,0:T(8,128)(2,1)} %constant.10.clone.mirror, ...), custom_call_target="tpu_custom_call" | custom-call | tf_op jit(solution)/shard_map/scores/pallas_call | solution.py:380
  116.8 1.5 %copy.10 = f32[96,192]{1,0:T(8,128)} copy(f32[96,192]{1,0:T(8,128)} %scores.1) | data formatting | bytes 147456

commit v5 on v4

--- a/solution.py
+++ b/solution.py
@@ -82,8 +82,8 @@
 
 
 OTHERS = [
-    (1, 2, 0), (0, 1, 0), (0, 3, 0), (1, 0, 0), (0, 2, 0), (1, 1, 1), (1, 3, 1), (1, 2, 1), (0, 1, 1), (0, 3, 1),
-    (1, 0, 1), (0, 2, 1), (1, 1, 0), (1, 3, 0), (0, 0, 1),
+    (1, 2, 0), (1, 2, 1), (0, 2, 0), (0, 2, 1), (1, 1, 0), (1, 3, 0), (1, 1, 1), (1, 3, 1),
+    (0, 1, 0), (0, 3, 0), (0, 1, 1), (0, 3, 1), (1, 0, 0), (1, 0, 1), (0, 0, 1),
 ]
 
 
@@ -292,12 +292,15 @@
             @pl.when(s == group * GROUP)
             def _():
                 take(group)
-                if group + EARLY < GROUPS:
-                    hand_over(group + EARLY)
 
         @pl.when(s < PARTS)
         def _():
-            start((0, 15, 1, 3, 16, 18, 7), s)
+            start((0, 1, 3, 15, 16, 18, 7), s)
+
+        for group in range(EARLY, GROUPS):
+            @pl.when(s == (group - EARLY) * GROUP + 1)
+            def _():
+                hand_over(group)
 
         @pl.when((s >= AHEAD) & (s < PARTS + AHEAD))
         def _():
@@ -362,11 +365,11 @@
         out[rows, :] = found / (math.sqrt(NX * ENTRIES) * scale * scale_col)
 
     def best(b, _):
-        for u in range(4):
-            some(b * 4 + u)
+        for u in range(6):
+            some(b * 6 + u)
         return 0
 
-    lax.fori_loop(0, 96 // 32, best, 0)
+    lax.fori_loop(0, 96 // 48, best, 0)
 
     for e, device in enumerate(others):
         tell(e, my_row, device).wait_send()

time: 119 us -> 118 us (level)
  no operation moved by 1% of the time
where the time goes in v5:
time: 118 us
  Pallas kernels  116 us (98%)
  local copies, waits for them, and re-layouts  1.54 us (1%)
    pallas_call x1, Pallas kernels, scores_of(): pl.pallas_call(score_kernel, out_shape=jax.ShapeDtypeStruct((COLS * M, RO...  116 us

profile of v5, /device:TPU:1, one launch (start us, length us, event | category | flops | bytes accessed | tf_op | source)
XLA Modules:
  0.0 117.8 jit_solution(15309189906736801640)
XLA Ops:
  0.7 115.6 %scores.1 = f32[96,192]{1,0:T(8,128)} custom-call(s32[1,1]{1,0:T(1,128)S(6)} %copy.9.count, s32[1,48]{1,0:T(1,128)} %dest.1, bf16[48,256,128]{2,1,0:T(8,128)(2,1)} %bitcast.1, bf16[384,128]{1,0:T(8,128)(2,1)} %constant.8.clone.forward, bf16[256,256]{1,0:T(8,128)(2,1)} %constant.9.clone.swap, bf16[256,256]{1,0:T(8,128)(2,1)} %constant.10.clone.mirror, ...), custom_call_target="tpu_custom_call" | custom-call | tf_op jit(solution)/shard_map/scores/pallas_call | solution.py:383
  116.3 1.5 %copy.10 = f32[96,192]{1,0:T(8,128)} copy(f32[96,192]{1,0:T(8,128)} %scores.1) | data formatting | bytes 147456
